TPU v7x, 32 devices: a whole 2x2x4 slice. The times are simulated.
32 devices in a mesh: seq: 8 (over z, x), ch: 4 (over y, core).
Axes of the slice: x: 2, y: 2, z: 4, core: 2. Of those that a mesh axis runs over, the one named last changes fastest.
Arguments:
- block_input: bfloat16 [8192, 2048], P('ch', 'seq'), may hold values from -110 to 110
- norm_gain: float32 [8192], P('ch'), may hold values from 0.1 to 1.9
- short_taps: bfloat16 [8192, 7], P('ch'), may hold values from -2 to 2
- medium_taps: bfloat16 [8192, 128], P('ch'), may hold values from -0.5 to 0.5
- long_filter: float32 [8192, 2048], P(('ch', 'seq')), may hold values from -2 to 2
- grad_out: bfloat16 [8192, 2048], P('ch', 'seq'), may hold values from -2.390625 to 2.390625
Outputs:
- grad_normed: bfloat16 [8192, 2048], P('ch', 'seq')
- grad_long: float32 [8192, 2048], P(('ch', 'seq'))
- grad_medium: float32 [8192, 128], P(('ch', 'seq'))
- grad_short: float32 [8192, 7], P(('ch', 'seq'))
All inputs are finite; a program needn't handle non-finite values.
Results may differ from a plain program's by a relative error of at most 0.0058.
Values may be sent and summed in bfloat16 or wider, within the bound.
A program may use at most 128 MiB of HBM per device.

v0:
```python
import math
import jax
import jax.numpy as jnp
from jax import lax
from jax.sharding import PartitionSpec as P

highest = lax.Precision.HIGHEST


def depthwise(signal, taps):
    result = lax.conv_general_dilated(
        signal[None],
        taps[:, None, :],
        (1,),
        "VALID",
        dimension_numbers=("NCH", "OIH", "NCH"),
        feature_group_count=signal.shape[0],
        preferred_element_type=jnp.float32,
    )
    return result[0]


def fourier_tables(length):
    total = 2 * length
    inner = 128
    outer = total // inner
    half = outer // 2
    two_pi = 2.0 * math.pi
    freq_outer = jnp.arange(outer, dtype=jnp.int32)
    pos_half = jnp.arange(half, dtype=jnp.int32)
    pos_inner = jnp.arange(inner, dtype=jnp.int32)
    outer_angle = (
        two_pi * (freq_outer[:, None] * pos_half[None, :] % outer).astype(jnp.float32) / outer
    )
    inner_angle = (
        two_pi * (pos_inner[:, None] * pos_inner[None, :] % inner).astype(jnp.float32) / inner
    )
    twist_angle = (
        two_pi * (freq_outer[:, None] * pos_inner[None, :] % total).astype(jnp.float32) / total
    )
    return (
        jnp.cos(outer_angle),
        jnp.sin(outer_angle),
        jnp.cos(inner_angle),
        jnp.sin(inner_angle),
        jnp.cos(twist_angle),
        jnp.sin(twist_angle),
    )


def forward_dft(signal, tables):
    cos_outer, sin_outer, cos_inner, sin_inner, cos_twist, sin_twist = tables
    blocks = signal.reshape(signal.shape[0], cos_outer.shape[1], cos_inner.shape[0])
    real = jnp.einsum("kn,cnq->ckq", cos_outer, blocks, precision=highest)
    imag = -jnp.einsum("kn,cnq->ckq", sin_outer, blocks, precision=highest)
    turned_re = real * cos_twist + imag * sin_twist
    turned_im = imag * cos_twist - real * sin_twist
    out_re = jnp.einsum("ckq,qr->ckr", turned_re, cos_inner, precision=highest) + jnp.einsum(
        "ckq,qr->ckr", turned_im, sin_inner, precision=highest
    )
    out_im = jnp.einsum("ckq,qr->ckr", turned_im, cos_inner, precision=highest) - jnp.einsum(
        "ckq,qr->ckr", turned_re, sin_inner, precision=highest
    )
    return (out_re, out_im)


def inverse_dft(spec_re, spec_im, tables):
    cos_outer, sin_outer, cos_inner, sin_inner, cos_twist, sin_twist = tables
    total = cos_outer.shape[0] * cos_inner.shape[0]
    step_re = jnp.einsum("ckq,qr->ckr", spec_re, cos_inner, precision=highest) - jnp.einsum(
        "ckq,qr->ckr", spec_im, sin_inner, precision=highest
    )
    step_im = jnp.einsum("ckq,qr->ckr", spec_im, cos_inner, precision=highest) + jnp.einsum(
        "ckq,qr->ckr", spec_re, sin_inner, precision=highest
    )
    turned_re = step_re * cos_twist - step_im * sin_twist
    turned_im = step_im * cos_twist + step_re * sin_twist
    blocks = jnp.einsum("kn,ckq->cnq", cos_outer, turned_re, precision=highest) - jnp.einsum(
        "kn,ckq->cnq", sin_outer, turned_im, precision=highest
    )
    return (blocks / total).reshape(spec_re.shape[0], -1)


def on_device(block_input, norm_gain, short_taps, medium_taps, long_filter, grad_out):
    chans, tokens = block_input.shape
    seq_count = lax.axis_size("seq")
    med_count = medium_taps.shape[1]
    reach = med_count + short_taps.shape[1] - 2
    inputs32 = block_input.astype(jnp.float32)
    squares = lax.psum(jnp.sum(inputs32 * inputs32, axis=0), "ch")
    inv_rms = lax.rsqrt(squares / (chans * lax.axis_size("ch")) + 1e-05)
    normed = (inputs32 * inv_rms[None, :] * norm_gain[:, None]).astype(jnp.bfloat16)
    arrived, grad_chan = (
        lax.all_to_all(normed, "seq", split_axis=0, concat_axis=1, tiled=True),
        lax.all_to_all(grad_out, "seq", split_axis=0, concat_axis=1, tiled=True),
    )
    group, length = arrived.shape
    scale = length ** (-0.5)
    offset = lax.axis_index("seq") * group
    short_local = lax.dynamic_slice_in_dim(short_taps, offset, group, 0)
    medium_local = lax.dynamic_slice_in_dim(medium_taps, offset, group, 0)
    normed_pad = jnp.pad(arrived, ((0, 0), (reach, 0)))
    shorted_pad = depthwise(normed_pad, short_local[:, ::-1]).astype(jnp.bfloat16)
    filtered_chan = depthwise(shorted_pad, medium_local[:, ::-1]).astype(jnp.bfloat16)
    tables = fourier_tables(length)
    grad_re, grad_im = forward_dft(grad_chan.astype(jnp.float32), tables)
    filt_re, filt_im = forward_dft(long_filter, tables)
    sig_re, sig_im = forward_dft(filtered_chan.astype(jnp.float32), tables)
    grad_filtered = inverse_dft(
        filt_re * grad_re + filt_im * grad_im, filt_re * grad_im - filt_im * grad_re, tables
    ).astype(jnp.bfloat16)
    grad_long = (
        inverse_dft(
            sig_re * grad_re + sig_im * grad_im, sig_re * grad_im - sig_im * grad_re, tables
        )
        * scale
    )
    back_pad = jnp.pad(grad_filtered, ((0, 0), (0, reach)))
    shorted_grad = depthwise(back_pad, medium_local).astype(jnp.bfloat16)
    normed_grad = depthwise(shorted_grad, short_local).astype(jnp.bfloat16)
    medium_local_grad = depthwise(shorted_pad, grad_filtered)[:, ::-1] * scale
    short_local_grad = (
        depthwise(normed_pad[:, med_count - 1 :], shorted_grad[:, :length])[:, ::-1] * scale
    )
    leaving = normed_grad.reshape(group, seq_count, tokens)
    returned = lax.all_to_all(leaving, "seq", split_axis=1, concat_axis=0, tiled=True).reshape(
        chans, -1
    )
    return (returned, grad_long, medium_local_grad, short_local_grad)


def solution(mesh):
    placed = (
        P("ch", "seq"),
        P("ch"),
        P("ch", None),
        P("ch", None),
        P(("ch", "seq"), None),
        P("ch", "seq"),
    )
    return jax.shard_map(
        on_device,
        mesh=mesh,
        in_specs=placed,
        out_specs=(
            P("ch", "seq"),
            P(("ch", "seq"), None),
            P(("ch", "seq"), None),
            P(("ch", "seq"), None),
        ),
        check_vma=False,
    )
```

profile of v0, /device:TPU:0, one launch (start us, length us, event | category | flops | bytes accessed | tf_op | source)
XLA Modules:
  0.0 433.6 jit_solution(14907793232586408200)
XLA Ops:
  2.2 8.4 %psum.7 = f32[256]{0:T(256)S(1)} all-reduce(f32[256]{0:T(256)S(1)} %fusion.44), channel_id=1, replica_groups=mesh['seq'=8,'ch'=4] {'ch'}, use_global_device_ids=true, to_apply=%region_1.0 | all-reduce | flops 256 | bytes 2048 | tf_op jit(solution)/shard_map/psum | solution.py:90
  34.9 9.3 %all-to-all-done.2 = bf16[8,256,256]{1,2,0:T(8,128)(2,1)} async-done(((bf16[8,256,256]{1,2,0:T(8,128)(2,1)}), bf16[8,256,256]{1,2,0:T(8,128)(2,1)}, u32[]{:S(2)}, u32[]{:S(2)}) %all-to-all-start.2) | async-done | bytes 1048608 | tf_op jit(solution)/shard_map/all_to_all | solution.py:94
  54.4 24.1 %fusion.66 = bf16[8,273,256]{2,0,1:T(8,128)(2,1)S(1)} fusion(bf16[256,1,128]{0,1,2:T(2,128)(2,1)S(1)} %copy.126, bf16[1,7,127,256]{3,1,2,0:T(8,128)(2,1)S(1)} %slice.20, bf16[1,8,273,256]{3,1,2,0:T(8,128)(2,1)S(1)} %select_bitcast_fusion), kind=kOutput, calls=%fused_computation.86 | convolution fusion | flops 148604928 | bytes 2757120 | tf_op jit(solution)/shard_map/conv_general_dilated | solution.py:11
  96.1 6.0 %add_bitcast_fusion = (f32[256,32,128]{2,1,0:T(8,128)S(1)}, f32[256,32,128]{2,1,0:T(8,128)S(1)}, f32[256,32,128]{2,1,0:T(8,128)S(1)}, f32[256,32,128]{2,1,0:T(8,128)S(1)}) fusion(f32[32,256,128]{2,0,1:T(8,128)S(1)} %fusion.161, f32[32,128]{1,0:T(8,128)S(1)} %get-tuple-element.38, f32[32,128]{1,0:T(8,128)S(1)} %get-tuple-element.39, ...), kind=kOutput, calls=%fused_computation.24 | convolution fusion | flops 216013824 | bytes 30441472 | tf_op jit(solution)/shard_map/kn,cnq->ckq/dot_general | solution.py:54
  102.1 8.6 %fusion.12 = f32[256,32,128]{2,0,1:T(8,128)} fusion(f32[256,32,128]{2,1,0:T(8,128)S(1)} %get-tuple-element.29), kind=kOutput, calls=%fused_computation.29 | convolution fusion | flops 1610842112 | bytes 8388608 | tf_op jit(solution)/shard_map/ckq,qr->ckr/dot_general | solution.py:58
  110.7 6.8 %fusion.10 = f32[256,32,128]{2,0,1:T(8,128)S(1)} fusion(f32[256,32,128]{2,1,0:T(8,128)S(1)} %get-tuple-element.29), kind=kOutput, calls=%fused_computation.27 | convolution fusion | flops 1610842112 | bytes 8388608 | tf_op jit(solution)/shard_map/ckq,qr->ckr/dot_general | solution.py:61
  117.5 7.2 %fusion.18 = f32[256,32,128]{2,0,1:T(8,128)S(1)} fusion(f32[256,32,128]{2,1,0:T(8,128)S(1)} %get-tuple-element.36), kind=kOutput, calls=%fused_computation.35 | convolution fusion | flops 1610842112 | bytes 8388608 | tf_op jit(solution)/shard_map/ckq,qr->ckr/dot_general | solution.py:61
  124.7 7.1 %fusion.20 = f32[256,32,128]{2,0,1:T(8,128)S(1)} fusion(f32[256,32,128]{2,1,0:T(8,128)S(1)} %get-tuple-element.36), kind=kOutput, calls=%fused_computation.37 | convolution fusion | flops 1610842112 | bytes 8388608 | tf_op jit(solution)/shard_map/ckq,qr->ckr/dot_general | solution.py:58
  131.8 13.2 %fusion.92 = f32[256,32,128]{2,0,1:T(8,128)} fusion(f32[256,128,32]{1,2,0:T(8,128)S(1)} %copy-done.2, f32[256,128,32]{1,2,0:T(8,128)S(1)} %copy-done.3, f32[32,128]{1,0:T(8,128)S(1)} %get-tuple-element.38, f32[32,128]{1,0:T(8,128)S(1)} %get-tuple-element.39), kind=kOutput, calls=%fused_computation.109 | convolution fusion | flops 1615036416 | bytes 12615680 | tf_op jit(solution)/shard_map/ckq,qr->ckr/dot_general | solution.py:58
  145.0 12.9 %fusion.88 = f32[256,32,128]{2,0,1:T(8,128)} fusion(f32[256,128,32]{1,2,0:T(8,128)S(1)} %copy-done.2, f32[256,128,32]{1,2,0:T(8,128)S(1)} %copy-done.3, f32[32,128]{1,0:T(8,128)S(1)} %get-tuple-element.38, f32[32,128]{1,0:T(8,128)S(1)} %get-tuple-element.39), kind=kOutput, calls=%fused_computation.108 | convolution fusion | flops 1615036416 | bytes 12615680 | tf_op jit(solution)/shard_map/ckq,qr->ckr/dot_general | solution.py:61
  159.2 14.5 %convolution_add_fusion.1 = f32[256,32,128]{2,0,1:T(8,128)} fusion(f32[256,32,128]{2,0,1:T(8,128)} %fusion.92, f32[256,128,32]{1,2,0:T(8,128)S(1)} %copy-done.2, f32[256,128,32]{1,2,0:T(8,128)S(1)} %copy-done.3, f32[32,128]{1,0:T(8,128)S(1)} %get-tuple-element.38, f32[32,128]{1,0:T(8,128)S(1)} %get-tuple-element.39), kind=kOutput, calls=%fused_computation.62 | convolution fusion | flops 1616084992 | bytes 16809984 | tf_op jit(solution)/shard_map/ckq,qr->ckr/dot_general | solution.py:58
  173.7 8.4 %fusion.36 = f32[256,32,128]{2,0,1:T(8,128)} fusion(f32[256,32,128]{2,0,1:T(8,128)S(1)} %copy-done.8, f32[256,32,128]{2,1,0:T(8,128)S(1)} %get-tuple-element.28), kind=kOutput, calls=%fused_computation.57 | convolution fusion | flops 1611890688 | bytes 12582912 | tf_op jit(solution)/shard_map/ckq,qr->ckr/dot_general | solution.py:58
  182.1 8.6 %fusion.39 = f32[256,32,128]{2,0,1:T(8,128)} fusion(f32[256,32,128]{2,0,1:T(8,128)S(1)} %fusion.10, f32[256,32,128]{2,1,0:T(8,128)S(1)} %get-tuple-element.28), kind=kOutput, calls=%fused_computation.58 | convolution fusion | flops 1611890688 | bytes 12582912 | tf_op jit(solution)/shard_map/ckq,qr->ckr/dot_general | solution.py:61
  190.7 8.6 %fusion.33 = f32[256,32,128]{2,0,1:T(8,128)} fusion(f32[256,32,128]{2,0,1:T(8,128)S(1)} %fusion.18, f32[256,32,128]{2,1,0:T(8,128)S(1)} %get-tuple-element.37), kind=kOutput, calls=%fused_computation.56 | convolution fusion | flops 1611890688 | bytes 12582912 | tf_op jit(solution)/shard_map/ckq,qr->ckr/dot_general | solution.py:61
  199.3 8.4 %fusion.30 = f32[256,32,128]{2,0,1:T(8,128)} fusion(f32[256,32,128]{2,0,1:T(8,128)S(1)} %fusion.20, f32[256,32,128]{2,1,0:T(8,128)S(1)} %get-tuple-element.37), kind=kOutput, calls=%fused_computation.55 | convolution fusion | flops 1611890688 | bytes 12582912 | tf_op jit(solution)/shard_map/ckq,qr->ckr/dot_general | solution.py:58
  207.7 22.7 %multiply_subtract_fusion.1 = (f32[256,32,128]{2,0,1:T(8,128)}, f32[256,32,128]{2,0,1:T(8,128)}, f32[256,32,128]{2,0,1:T(8,128)}, f32[256,32,128]{2,0,1:T(8,128)}) fusion(f32[256,32,128]{2,0,1:T(8,128)} %fusion.36, f32[256,32,128]{2,0,1:T(8,128)} %convolution_add_fusion.1, f32[256,32,128]{2,0,1:T(8,128)} %fusion.39, f32[256,32,128]{2,0,1:T(8,128)} %fusion.33, ...), kind=kOutput, calls=%fused_computation.17 | convolution fusion | flops 1628667904 | bytes 50364416 | tf_op jit(solution)/shard_map/ckq,qr->ckr/dot_general | solution.py:61
  263.3 11.6 %multiply_subtract_fusion = (f32[256,32,128]{2,0,1:T(8,128)}, f32[256,32,128]{2,0,1:T(8,128)}, f32[256,32,128]{2,0,1:T(8,128)}, f32[256,32,128]{2,0,1:T(8,128)}) fusion(f32[256,32,128]{2,0,1:T(8,128)S(1)} %convolution_subtract_fusion, f32[32,128]{1,0:T(8,128)S(1)} %get-tuple-element.38, f32[32,128]{1,0:T(8,128)S(1)} %get-tuple-element.39, ...), kind=kOutput, calls=%fused_computation.16 | convolution fusion | flops 1624473600 | bytes 37781504 | tf_op jit(solution)/shard_map/ckq,qr->ckr/dot_general | solution.py:73
  274.9 7.0 %fusion.6 = f32[256,128,16]{1,2,0:T(8,128)S(1)} fusion(f32[256,32,128]{2,0,1:T(8,128)} %get-tuple-element.34), kind=kOutput, calls=%fused_computation.11 | convolution fusion | flops 201333760 | bytes 6291456 | tf_op jit(solution)/shard_map/kn,ckq->cnq/dot_general | solution.py:78
  289.9 28.6 %select_convert_fusion.1 = bf16[8,273,256]{2,0,1:T(8,128)(2,1)S(1)} fusion(bf16[256,1,128]{0,1,2:T(2,128)(2,1)S(1)} %copy-done.14, bf16[256,1,7,127]{0,2,3,1:T(8,128)(2,1)S(1)} %slice.16, bf16[256,1,8,273]{0,2,3,1:T(8,128)(2,1)S(1)} %copy.117, pred[8,273]{0,1:T(8,128)(4,1)S(1)} %copy-done.15), kind=kOutput, calls=%fused_computation.54 | convolution fusion | flops 149164032 | bytes 2759304 | tf_op jit(solution)/shard_map/conv_general_dilated | solution.py:11
  330.6 6.8 %fusion.2 = f32[256,128,16]{1,2,0:T(8,128)S(1)} fusion(f32[256,32,128]{2,0,1:T(8,128)} %get-tuple-element.25), kind=kOutput, calls=%fused_computation.6 | convolution fusion | flops 201333760 | bytes 6291456 | tf_op jit(solution)/shard_map/kn,ckq->cnq/dot_general | solution.py:78
  337.5 6.5 %reshape.129 = bf16[1,2184,256]{2,0,1:T(2,128)(2,1)} reshape(bf16[8,273,256]{2,1,0:T(8,128)(2,1)} %copy.133) | data formatting | bytes 2236416 | tf_op jit(solution)/shard_map/convert_element_type | solution.py:103
  349.9 25.4 %fusion.326 = f32[1,256,128]{1,0,2:T(1,128)S(1)} fusion(bf16[1,2184,256]{2,0,1:T(2,128)(2,1)} %reshape.129, bf16[256,1,2048]{0,1,2:T(2,128)(2,1)} %copy.135), kind=kOutput, calls=%fused_computation.326 | convolution fusion | flops 134217728 | bytes 2297856 | tf_op jit(solution)/shard_map/conv_general_dilated | solution.py:11
  380.3 6.9 %subtract_multiply_fusion = f32[256,128,16]{1,2,0:T(8,128)S(1)} fusion(f32[256,128,16]{1,2,0:T(8,128)S(1)} %fusion.2, f32[256,32,128]{2,0,1:T(8,128)} %get-tuple-element.24), kind=kOutput, calls=%fused_computation.72 | convolution fusion | flops 202382336 | bytes 8388608 | tf_op jit(solution)/shard_map/kn,ckq->cnq/dot_general | solution.py:78
  391.8 38.4 %fusion.42 = f32[1,256,7]{1,0,2:T(1,128)S(1)} fusion(bf16[1,256,2054]{1,2,0:T(8,128)(2,1)S(1)} %slice_bitcast_fusion.1, bf16[256,1,2048]{0,2,1:T(8,128)(2,1)S(1)} %slice_bitcast_fusion.2), kind=kOutput, calls=%fused_computation.65 | convolution fusion | flops 7340032 | bytes 2107392 | tf_op jit(solution)/shard_map/conv_general_dilated | solution.py:11
  (111 shorter events, 125.8 us)
Async XLA Ops:
  0.6 18.7 %copy-start = (bf16[2048,128]{1,0:T(8,128)(2,1)S(1)}, bf16[2048,128]{1,0:T(8,128)(2,1)}, u32[]{:S(2)}) copy-start(bf16[2048,128]{1,0:T(8,128)(2,1)} %param.9) | copy-start | bytes 1572868
  13.5 30.7 %all-to-all-start.2 = ((bf16[8,256,256]{1,2,0:T(8,128)(2,1)}), bf16[8,256,256]{1,2,0:T(8,128)(2,1)}, u32[]{:S(2)}, u32[]{:S(2)}) async-start(bf16[8,256,256]{1,2,0:T(8,128)(2,1)} %copy.122), calls=%async_computation.2 | async-start | bytes 2097152 | tf_op jit(solution)/shard_map/all_to_all | solution.py:94
  44.2 45.7 %all-to-all-start = ((bf16[8,256,256]{2,1,0:T(8,128)(2,1)}), bf16[8,256,256]{2,1,0:T(8,128)(2,1)}, u32[]{:S(2)}, u32[]{:S(2)}) async-start(bf16[8,256,256]{2,1,0:T(8,128)(2,1)} %bitcast.210), calls=%async_computation | async-start | bytes 2097152 | tf_op jit(solution)/shard_map/all_to_all | solution.py:95
  48.4 2.2 copy-start.16
  53.4 25.2 %copy-start.11 = (bf16[8,273,256]{2,0,1:T(8,128)(2,1)}, bf16[8,273,256]{2,0,1:T(8,128)(2,1)S(1)}, u32[]{:S(2)}) copy-start(bf16[8,273,256]{2,0,1:T(8,128)(2,1)S(1)} %select_convert_fusion) | copy-start | bytes 3354628
  92.8 3.3 copy-start.9
  124.7 7.1 %copy-start.2 = (f32[256,128,32]{1,2,0:T(8,128)S(1)}, f32[256,128,32]{1,2,0:T(8,128)}, u32[]{:S(2)}) copy-start(f32[256,128,32]{1,2,0:T(8,128)} %fusion.166) | copy-start | bytes 12582916
  124.7 7.1 %copy-start.3 = (f32[256,128,32]{1,2,0:T(8,128)S(1)}, f32[256,128,32]{1,2,0:T(8,128)}, u32[]{:S(2)}) copy-start(f32[256,128,32]{1,2,0:T(8,128)} %fusion.158) | copy-start | bytes 12582916
  145.0 12.9 %copy-start.12 = (bf16[8,273,256]{2,0,1:T(8,128)(2,1)S(1)}, bf16[8,273,256]{2,0,1:T(8,128)(2,1)}, u32[]{:S(2)}) copy-start(bf16[8,273,256]{2,0,1:T(8,128)(2,1)} %copy-done.11) | copy-start | bytes 3354628
  159.2 14.5 %copy-start.8 = (f32[256,32,128]{2,0,1:T(8,128)S(1)}, f32[256,32,128]{2,0,1:T(8,128)}, u32[]{:S(2)}) copy-start(f32[256,32,128]{2,0,1:T(8,128)} %fusion.12) | copy-start | bytes 12582916
  230.4 6.0 %copy-start.6 = (f32[256,32,128]{2,0,1:T(8,128)S(1)}, f32[256,32,128]{2,0,1:T(8,128)}, u32[]{:S(2)}) copy-start(f32[256,32,128]{2,0,1:T(8,128)} %get-tuple-element.20) | copy-start | bytes 12582916
  242.1 3.8 copy-start.4
  245.9 3.8 copy-start.5
  257.7 5.6 %copy-start.7 = (f32[256,32,128]{2,0,1:T(8,128)S(1)}, f32[256,32,128]{2,0,1:T(8,128)}, u32[]{:S(2)}) copy-start(f32[256,32,128]{2,0,1:T(8,128)} %get-tuple-element.21) | copy-start | bytes 12582916
  274.9 7.0 %copy-start.10 = (f32[256,32,128]{2,0,1:T(8,128)S(1)}, f32[256,32,128]{2,0,1:T(8,128)}, u32[]{:S(2)}) copy-start(f32[256,32,128]{2,0,1:T(8,128)} %get-tuple-element.35) | copy-start | bytes 12582916
  289.0 0.9 copy-start.14
  289.0 0.9 copy-start.15
  318.5 2.2 copy-start.17
  324.7 106.2 %all-to-all-start.1 = ((bf16[256,8,256]{0,2,1:T(8,128)(2,1)}), bf16[256,8,256]{0,2,1:T(8,128)(2,1)}, u32[]{:S(2)}, u32[]{:S(2)}) async-start(bf16[256,8,256]{0,2,1:T(8,128)(2,1)} %bitcast.19), calls=%async_computation.1 | async-start | bytes 2097152 | tf_op jit(solution)/shard_map/all_to_all | solution.py:126
  387.2 4.5 %copy-start.13 = (bf16[256,2054]{0,1:T(8,128)(2,1)S(1)}, bf16[256,2054]{0,1:T(8,128)(2,1)}, u32[]{:S(2)}) copy-start(bf16[256,2054]{0,1:T(8,128)(2,1)} %slice_bitcast_fusion) | copy-start | bytes 3154948
  391.8 41.4 %copy-start.1 = (bf16[2048,128]{1,0:T(8,128)(2,1)S(1)}, bf16[2048,128]{1,0:T(8,128)(2,1)}, u32[]{:S(2)}) copy-start(bf16[2048,128]{1,0:T(8,128)(2,1)} %param.9) | copy-start | bytes 1572868
where the time goes:
time: 440 us; the launch traced here: 434 us
  matrix products  346 us (79%)
  local copies, waits for them, and re-layouts  46.6 us (11%)
  starting transfers between devices  15.9 us (4%)
  waiting for transfers between devices  9.3 us (2%)
  blocking collectives  8.36 us (2%)
  other arithmetic  5.68 us (1%)
    conv_general_dilated x6, matrix products, depthwise(): lax.conv_general_dilated(signal[None], taps[:, None, :], (1,), 'VALID', d...  122 us
    dot_general x3, matrix products, forward_dft(): jnp.einsum('ckq,qr->ckr', turned_re, sin_inner, precision=highest)  39.9 us
    dot_general x3, matrix products, forward_dft(): jnp.einsum('ckq,qr->ckr', turned_im, sin_inner, precision=highest)  30.2 us
    dot_general x3, matrix products, forward_dft(): jnp.einsum('ckq,qr->ckr', turned_re, cos_inner, precision=highest)  30 us
    dot_general x3, matrix products, forward_dft(): jnp.einsum('ckq,qr->ckr', turned_im, cos_inner, precision=highest)  26.9 us
    dot_general x2, matrix products, inverse_dft(): jnp.einsum('ckq,qr->ckr', spec_re, sin_inner, precision=highest)  17.2 us
    dot_general x3, matrix products, forward_dft(): real = jnp.einsum('kn,cnq->ckq', cos_outer, blocks, precision=highest)  15 us
    dot_general x2, matrix products, inverse_dft(): jnp.einsum('kn,ckq->cnq', sin_outer, turned_im, precision=highest)  13.8 us
  transfers between devices with their start and end apart: 3, of which 1 were waited for; matrix products, arithmetic and copies ran while one was open for 36% of the time, Pallas kernels for 0%

commit v1 on v0

--- a/solution.py
+++ b/solution.py
@@ -5,6 +5,28 @@
 from jax.sharding import PartitionSpec as P
 
 highest = lax.Precision.HIGHEST
+
+
+def in_blocks(x, dim, count):
+    before, after = (x.shape[:dim], x.shape[dim + 1 :])
+    return jnp.moveaxis(x.reshape(*before, count, -1, *after), dim, 0)
+
+
+def in_order(blocks, dim):
+    shape = list(blocks.shape[1:])
+    shape[dim] *= blocks.shape[0]
+    return jnp.moveaxis(blocks, 0, dim).reshape(shape)
+
+
+def pairwise_exchange(x, axis, split_dim, concat_dim):
+    devices, place = (lax.axis_size(axis), lax.axis_index(axis))
+    blocks = in_blocks(x, split_dim, devices)
+    finished = [blocks[place]]
+    for turn in range(1, devices):
+        sent = blocks[place ^ turn]
+        finished.append(lax.ppermute(sent, axis, [(i, i ^ turn) for i in range(devices)]))
+    blocks = jnp.stack(finished)[place ^ jnp.arange(devices)]
+    return in_order(blocks, concat_dim)
 
 
 def depthwise(signal, taps):
@@ -91,7 +113,7 @@
     inv_rms = lax.rsqrt(squares / (chans * lax.axis_size("ch")) + 1e-05)
     normed = (inputs32 * inv_rms[None, :] * norm_gain[:, None]).astype(jnp.bfloat16)
     arrived, grad_chan = (
-        lax.all_to_all(normed, "seq", split_axis=0, concat_axis=1, tiled=True),
+        pairwise_exchange(normed, "seq", 0, 1),
         lax.all_to_all(grad_out, "seq", split_axis=0, concat_axis=1, tiled=True),
     )
     group, length = arrived.shape

time: 440 us -> 428 us (0.973)
  matrix products: 346 us -> 332 us
  starting transfers between devices: 15.9 us -> 24.2 us
  waiting for transfers between devices: 9.3 us -> 4.17 us
    ppermute x0 -> x7, starting transfers between devices: none -> 11.2 us  [pairwise_exchange(): lax.ppermute(sent, axis, [(i, i ^ turn) for i in range(devices)])]
    conv_general_dilated x6, matrix products: 122 us -> 112 us  [depthwise(): lax.conv_general_dilated(signal[None], taps[:, None, :], (1,), 'VALID', d...]
    all_to_all x1 -> x0, waiting for transfers between devices: 9.3 us -> none  [on_device(): lax.all_to_all(normed, 'seq', split_axis=0, concat_axis=1, tiled=True)]
    all_to_all x1 -> x0, starting transfers between devices: 5.81 us -> none  [on_device(): lax.all_to_all(normed, 'seq', split_axis=0, concat_axis=1, tiled=True)]
    convert_element_type x4, local copies, waits for them, and re-layouts: 6.09 us -> 0.64 us  [on_device(): shorted_grad = depthwise(back_pad, medium_local).astype(jnp.bfloat16)]
    unnamed x41 -> x43, local copies, waits for them, and re-layouts: 5.13 us -> 9.11 us
  transfers between devices with their start and end apart: 3 -> 9, of which waited for: 1 -> 2; matrix products, arithmetic and copies ran while one was open for 36% -> 45% of each run, Pallas kernels for 0% -> 0%
where the time goes in v1:
time: 428 us; the launch traced here: 420 us
  matrix products  332 us (78%)
  local copies, waits for them, and re-layouts  45.7 us (11%)
  starting transfers between devices  24.2 us (6%)
  blocking collectives  6.72 us (2%)
  other arithmetic  5.63 us (1%)
    conv_general_dilated x6, matrix products, depthwise(): lax.conv_general_dilated(signal[None], taps[:, None, :], (1,), 'VALID', d...  112 us
    dot_general x3, matrix products, forward_dft(): jnp.einsum('ckq,qr->ckr', turned_re, sin_inner, precision=highest)  39.4 us
    dot_general x3, matrix products, forward_dft(): jnp.einsum('ckq,qr->ckr', turned_re, cos_inner, precision=highest)  31.7 us
    dot_general x3, matrix products, forward_dft(): jnp.einsum('ckq,qr->ckr', turned_im, cos_inner, precision=highest)  27.2 us
    dot_general x3, matrix products, forward_dft(): jnp.einsum('ckq,qr->ckr', turned_im, sin_inner, precision=highest)  26.9 us
    dot_general x2, matrix products, inverse_dft(): jnp.einsum('ckq,qr->ckr', spec_re, sin_inner, precision=highest)  17.2 us
    dot_general x3, matrix products, forward_dft(): real = jnp.einsum('kn,cnq->ckq', cos_outer, blocks, precision=highest)  15 us
    dot_general x2, matrix products, inverse_dft(): jnp.einsum('kn,ckq->cnq', sin_outer, turned_im, precision=highest)  14 us
  transfers between devices with their start and end apart: 9, of which 2 were waited for; matrix products, arithmetic and copies ran while one was open for 45% of the time, Pallas kernels for 0%

profile of v1, /device:TPU:0, one launch (start us, length us, event | category | flops | bytes accessed | tf_op | source)
XLA Modules:
  0.0 420.4 jit_solution(4408019492440649438)
XLA Ops:
  0.6 7.4 %all-to-all-start = ((bf16[8,256,256]{2,1,0:T(8,128)(2,1)}), bf16[8,256,256]{2,1,0:T(8,128)(2,1)}, u32[]{:S(2)}, u32[]{:S(2)}) async-start(bf16[8,256,256]{2,1,0:T(8,128)(2,1)} %bitcast.242), calls=%async_computation | async-start | bytes 2097152 | tf_op jit(solution)/shard_map/all_to_all | solution.py:117
  9.6 6.7 %psum.7 = f32[256]{0:T(256)S(1)} all-reduce(f32[256]{0:T(256)S(1)} %fusion.44), channel_id=1, replica_groups=mesh['seq'=8,'ch'=4] {'ch'}, use_global_device_ids=true, to_apply=%region_1.0 | all-reduce | flops 256 | bytes 2048 | tf_op jit(solution)/shard_map/psum | solution.py:112
  62.7 24.1 %fusion.66 = bf16[8,273,256]{2,0,1:T(8,128)(2,1)S(1)} fusion(bf16[256,1,128]{0,1,2:T(2,128)(2,1)S(1)} %copy.124, bf16[1,7,127,256]{3,1,2,0:T(8,128)(2,1)S(1)} %slice.22, bf16[1,8,273,256]{3,1,2,0:T(8,128)(2,1)S(1)} %select_bitcast_fusion), kind=kOutput, calls=%fused_computation.87 | convolution fusion | flops 148604928 | bytes 2757120 | tf_op jit(solution)/shard_map/conv_general_dilated | solution.py:33
  104.8 14.1 %fusion.92 = f32[256,32,128]{2,0,1:T(8,128)S(1)} fusion(f32[256,128,32]{1,2,0:T(8,128)} %fusion.166, f32[256,128,32]{1,2,0:T(8,128)} %fusion.158, f32[32,128]{1,0:T(8,128)S(1)} %get-tuple-element.46, f32[32,128]{1,0:T(8,128)S(1)} %get-tuple-element.47), kind=kOutput, calls=%fused_computation.110 | convolution fusion | flops 1615036416 | bytes 12615680 | tf_op jit(solution)/shard_map/ckq,qr->ckr/dot_general | solution.py:80
  118.9 13.0 %fusion.88 = f32[256,32,128]{2,0,1:T(8,128)} fusion(f32[256,128,32]{1,2,0:T(8,128)S(1)} %copy-done.2, f32[256,128,32]{1,2,0:T(8,128)S(1)} %copy-done.3, f32[32,128]{1,0:T(8,128)S(1)} %get-tuple-element.46, f32[32,128]{1,0:T(8,128)S(1)} %get-tuple-element.47), kind=kOutput, calls=%fused_computation.109 | convolution fusion | flops 1615036416 | bytes 12615680 | tf_op jit(solution)/shard_map/ckq,qr->ckr/dot_general | solution.py:83
  131.9 13.0 %convolution_add_fusion.1 = f32[256,32,128]{2,0,1:T(8,128)} fusion(f32[256,32,128]{2,0,1:T(8,128)S(1)} %fusion.92, f32[256,128,32]{1,2,0:T(8,128)S(1)} %copy-done.2, f32[256,128,32]{1,2,0:T(8,128)S(1)} %copy-done.3, f32[32,128]{1,0:T(8,128)S(1)} %get-tuple-element.46, f32[32,128]{1,0:T(8,128)S(1)} %get-tuple-element.47), kind=kOutput, calls=%fused_computation.63 | convolution fusion | flops 1616084992 | bytes 16809984 | tf_op jit(solution)/shard_map/ckq,qr->ckr/dot_general | solution.py:80
  151.5 6.0 %add_bitcast_fusion = (f32[256,32,128]{2,1,0:T(8,128)S(1)}, f32[256,32,128]{2,1,0:T(8,128)S(1)}, f32[256,32,128]{2,1,0:T(8,128)S(1)}, f32[256,32,128]{2,1,0:T(8,128)S(1)}) fusion(f32[32,256,128]{2,0,1:T(8,128)S(1)} %fusion.161, f32[32,128]{1,0:T(8,128)S(1)} %get-tuple-element.46, f32[32,128]{1,0:T(8,128)S(1)} %get-tuple-element.47, ...), kind=kOutput, calls=%fused_computation.25 | convolution fusion | flops 216013824 | bytes 30441472 | tf_op jit(solution)/shard_map/kn,cnq->ckq/dot_general | solution.py:76
  157.6 7.0 %fusion.12 = f32[256,32,128]{2,0,1:T(8,128)S(1)} fusion(f32[256,32,128]{2,1,0:T(8,128)S(1)} %get-tuple-element.29), kind=kOutput, calls=%fused_computation.30 | convolution fusion | flops 1610842112 | bytes 8388608 | tf_op jit(solution)/shard_map/ckq,qr->ckr/dot_general | solution.py:80
  164.6 7.0 %fusion.10 = f32[256,32,128]{2,0,1:T(8,128)S(1)} fusion(f32[256,32,128]{2,1,0:T(8,128)S(1)} %get-tuple-element.29), kind=kOutput, calls=%fused_computation.28 | convolution fusion | flops 1610842112 | bytes 8388608 | tf_op jit(solution)/shard_map/ckq,qr->ckr/dot_general | solution.py:83
  171.5 7.2 %fusion.18 = f32[256,32,128]{2,0,1:T(8,128)S(1)} fusion(f32[256,32,128]{2,1,0:T(8,128)S(1)} %get-tuple-element.44), kind=kOutput, calls=%fused_computation.36 | convolution fusion | flops 1610842112 | bytes 8388608 | tf_op jit(solution)/shard_map/ckq,qr->ckr/dot_general | solution.py:83
  178.8 7.0 %fusion.20 = f32[256,32,128]{2,0,1:T(8,128)S(1)} fusion(f32[256,32,128]{2,1,0:T(8,128)S(1)} %get-tuple-element.44), kind=kOutput, calls=%fused_computation.38 | convolution fusion | flops 1610842112 | bytes 8388608 | tf_op jit(solution)/shard_map/ckq,qr->ckr/dot_general | solution.py:80
  185.8 8.8 %fusion.36 = f32[256,32,128]{2,0,1:T(8,128)} fusion(f32[256,32,128]{2,0,1:T(8,128)S(1)} %fusion.12, f32[256,32,128]{2,1,0:T(8,128)S(1)} %get-tuple-element.28), kind=kOutput, calls=%fused_computation.58 | convolution fusion | flops 1611890688 | bytes 12582912 | tf_op jit(solution)/shard_map/ckq,qr->ckr/dot_general | solution.py:80
  194.6 8.5 %fusion.39 = f32[256,32,128]{2,0,1:T(8,128)} fusion(f32[256,32,128]{2,0,1:T(8,128)S(1)} %fusion.10, f32[256,32,128]{2,1,0:T(8,128)S(1)} %get-tuple-element.28), kind=kOutput, calls=%fused_computation.59 | convolution fusion | flops 1611890688 | bytes 12582912 | tf_op jit(solution)/shard_map/ckq,qr->ckr/dot_general | solution.py:83
  203.1 8.5 %fusion.33 = f32[256,32,128]{2,0,1:T(8,128)} fusion(f32[256,32,128]{2,0,1:T(8,128)S(1)} %fusion.18, f32[256,32,128]{2,1,0:T(8,128)S(1)} %get-tuple-element.45), kind=kOutput, calls=%fused_computation.57 | convolution fusion | flops 1611890688 | bytes 12582912 | tf_op jit(solution)/shard_map/ckq,qr->ckr/dot_general | solution.py:83
  211.6 8.7 %fusion.30 = f32[256,32,128]{2,0,1:T(8,128)} fusion(f32[256,32,128]{2,0,1:T(8,128)S(1)} %fusion.20, f32[256,32,128]{2,1,0:T(8,128)S(1)} %get-tuple-element.45), kind=kOutput, calls=%fused_computation.56 | convolution fusion | flops 1611890688 | bytes 12582912 | tf_op jit(solution)/shard_map/ckq,qr->ckr/dot_general | solution.py:80
  220.3 22.4 %multiply_subtract_fusion.1 = (f32[256,32,128]{2,0,1:T(8,128)}, f32[256,32,128]{2,0,1:T(8,128)}, f32[256,32,128]{2,0,1:T(8,128)}, f32[256,32,128]{2,0,1:T(8,128)}) fusion(f32[256,32,128]{2,0,1:T(8,128)} %fusion.36, f32[256,32,128]{2,0,1:T(8,128)} %convolution_add_fusion.1, f32[256,32,128]{2,0,1:T(8,128)} %fusion.39, f32[256,32,128]{2,0,1:T(8,128)} %fusion.33, ...), kind=kOutput, calls=%fused_computation.18 | convolution fusion | flops 1628667904 | bytes 50364416 | tf_op jit(solution)/shard_map/ckq,qr->ckr/dot_general | solution.py:83
  242.7 6.0 %fusion.111 = f32[256,32,128]{2,0,1:T(8,128)S(1)} fusion(f32[256,32,128]{2,0,1:T(8,128)} %get-tuple-element.21), kind=kOutput, calls=%fused_computation.147 | convolution fusion | flops 1610842112 | bytes 8388608 | tf_op jit(solution)/shard_map/ckq,qr->ckr/dot_general | solution.py:92
  248.7 5.8 %fusion.109 = f32[256,32,128]{2,0,1:T(8,128)} fusion(f32[256,32,128]{2,0,1:T(8,128)S(1)} %copy-done.6), kind=kOutput, calls=%fused_computation.145 | convolution fusion | flops 1610842112 | bytes 8388608 | tf_op jit(solution)/shard_map/ckq,qr->ckr/dot_general | solution.py:95
  275.6 11.6 %multiply_subtract_fusion = (f32[256,32,128]{2,0,1:T(8,128)}, f32[256,32,128]{2,0,1:T(8,128)}, f32[256,32,128]{2,0,1:T(8,128)}, f32[256,32,128]{2,0,1:T(8,128)}) fusion(f32[256,32,128]{2,0,1:T(8,128)S(1)} %convolution_subtract_fusion, f32[32,128]{1,0:T(8,128)S(1)} %get-tuple-element.46, f32[32,128]{1,0:T(8,128)S(1)} %get-tuple-element.47, ...), kind=kOutput, calls=%fused_computation.17 | convolution fusion | flops 1624473600 | bytes 37781504 | tf_op jit(solution)/shard_map/ckq,qr->ckr/dot_general | solution.py:95
  287.2 7.0 %fusion.6 = f32[256,128,16]{1,2,0:T(8,128)S(1)} fusion(f32[256,32,128]{2,0,1:T(8,128)} %get-tuple-element.42), kind=kOutput, calls=%fused_computation.12 | convolution fusion | flops 201333760 | bytes 6291456 | tf_op jit(solution)/shard_map/kn,ckq->cnq/dot_general | solution.py:100
  302.1 28.8 %select_convert_fusion.1 = bf16[8,273,256]{2,0,1:T(8,128)(2,1)S(1)} fusion(bf16[256,1,128]{0,1,2:T(2,128)(2,1)S(1)} %copy-done.12, bf16[256,1,7,127]{0,2,3,1:T(8,128)(2,1)S(1)} %slice.18, bf16[256,1,8,273]{0,2,3,1:T(8,128)(2,1)S(1)} %copy.115, pred[8,273]{0,1:T(8,128)(4,1)S(1)} %copy-done.13), kind=kOutput, calls=%fused_computation.55 | convolution fusion | flops 149164032 | bytes 2759304 | tf_op jit(solution)/shard_map/conv_general_dilated | solution.py:33
  343.8 7.0 %fusion.2 = f32[256,128,16]{1,2,0:T(8,128)S(1)} fusion(f32[256,32,128]{2,0,1:T(8,128)} %get-tuple-element.25), kind=kOutput, calls=%fused_computation.7 | convolution fusion | flops 201333760 | bytes 6291456 | tf_op jit(solution)/shard_map/kn,ckq->cnq/dot_general | solution.py:100
  361.7 25.4 %fusion.327 = f32[1,256,128]{1,0,2:T(1,128)S(1)} fusion(bf16[1,2184,256]{2,0,1:T(2,128)(2,1)} %reshape.158, bf16[256,1,2048]{0,1,2:T(2,128)(2,1)} %copy.133), kind=kOutput, calls=%fused_computation.345 | convolution fusion | flops 134217728 | bytes 2297856 | tf_op jit(solution)/shard_map/conv_general_dilated | solution.py:33
  388.7 28.6 %fusion.42 = f32[1,256,7]{1,0,2:T(1,128)S(1)} fusion(bf16[1,256,2054]{1,2,0:T(8,128)(2,1)} %slice_bitcast_fusion.1, bf16[256,1,2048]{0,2,1:T(8,128)(2,1)S(1)} %slice_bitcast_fusion.2), kind=kOutput, calls=%fused_computation.66 | convolution fusion | flops 7340032 | bytes 2107392 | tf_op jit(solution)/shard_map/conv_general_dilated | solution.py:33
  (130 shorter events, 129.3 us)
Async XLA Ops:
  0.6 37.9 %copy-start = (bf16[2048,128]{1,0:T(8,128)(2,1)S(1)}, bf16[2048,128]{1,0:T(8,128)(2,1)}, u32[]{:S(2)}) copy-start(bf16[2048,128]{1,0:T(8,128)(2,1)} %param.9) | copy-start | bytes 1572868
  0.6 144.2 %all-to-all-start = ((bf16[8,256,256]{2,1,0:T(8,128)(2,1)}), bf16[8,256,256]{2,1,0:T(8,128)(2,1)}, u32[]{:S(2)}, u32[]{:S(2)}) async-start(bf16[8,256,256]{2,1,0:T(8,128)(2,1)} %bitcast.242), calls=%async_computation | async-start | bytes 2097152 | tf_op jit(solution)/shard_map/all_to_all | solution.py:117
  18.7 23.2 %collective-permute-start = (bf16[256,256]{1,0:T(8,128)(2,1)S(1)}, bf16[256,256]{1,0:T(8,128)(2,1)S(1)}, u32[]{:S(2)}, u32[]{:S(2)}) collective-permute-start(bf16[256,256]{1,0:T(8,128)(2,1)S(1)} %get-tuple-element.40), channel_id=1, source_target_pairs={{0,4},{4,0},{8,12},{12,8},{16,20},{20,16},{24,28},{28,24},{1,5},{5... | collective-permute-start | bytes 393224 | tf_op jit(solution)/shard_map/ppermute | solution.py:27
  20.4 25.5 %collective-permute-start.1 = (bf16[256,256]{1,0:T(8,128)(2,1)S(1)}, bf16[256,256]{1,0:T(8,128)(2,1)S(1)}, u32[]{:S(2)}, u32[]{:S(2)}) collective-permute-start(bf16[256,256]{1,0:T(8,128)(2,1)S(1)} %get-tuple-element.39), channel_id=1, source_target_pairs={{0,8},{4,12},{8,0},{12,4},{16,24},{20,28},{24,16},{28,20},{1,9},{5... | collective-permute-start | bytes 393224 | tf_op jit(solution)/shard_map/ppermute | solution.py:27
  21.9 25.0 %collective-permute-start.2 = (bf16[256,256]{1,0:T(8,128)(2,1)S(1)}, bf16[256,256]{1,0:T(8,128)(2,1)S(1)}, u32[]{:S(2)}, u32[]{:S(2)}) collective-permute-start(bf16[256,256]{1,0:T(8,128)(2,1)S(1)} %get-tuple-element.38), channel_id=1, source_target_pairs={{0,12},{4,8},{8,4},{12,0},{16,28},{20,24},{24,20},{28,16},{1,13},{... | collective-permute-start | bytes 393224 | tf_op jit(solution)/shard_map/ppermute | solution.py:27
  22.2 25.3 %collective-permute-start.3 = (bf16[256,256]{1,0:T(8,128)(2,1)S(1)}, bf16[256,256]{1,0:T(8,128)(2,1)S(1)}, u32[]{:S(2)}, u32[]{:S(2)}) collective-permute-start(bf16[256,256]{1,0:T(8,128)(2,1)S(1)} %get-tuple-element.37), channel_id=1, source_target_pairs={{0,16},{4,20},{8,24},{12,28},{16,0},{20,4},{24,8},{28,12},{1,17},{... | collective-permute-start | bytes 393224 | tf_op jit(solution)/shard_map/ppermute | solution.py:27
  24.8 26.4 %collective-permute-start.4 = (bf16[256,256]{1,0:T(8,128)(2,1)S(1)}, bf16[256,256]{1,0:T(8,128)(2,1)S(1)}, u32[]{:S(2)}, u32[]{:S(2)}) collective-permute-start(bf16[256,256]{1,0:T(8,128)(2,1)S(1)} %get-tuple-element.36), channel_id=1, source_target_pairs={{0,20},{4,16},{8,28},{12,24},{16,4},{20,0},{24,12},{28,8},{1,21},{... | collective-permute-start | bytes 393224 | tf_op jit(solution)/shard_map/ppermute | solution.py:27
  41.9 9.9 %collective-permute-start.5 = (bf16[256,256]{1,0:T(8,128)(2,1)S(1)}, bf16[256,256]{1,0:T(8,128)(2,1)S(1)}, u32[]{:S(2)}, u32[]{:S(2)}) collective-permute-start(bf16[256,256]{1,0:T(8,128)(2,1)S(1)} %get-tuple-element.35), channel_id=1, source_target_pairs={{0,24},{4,28},{8,16},{12,20},{16,8},{20,12},{24,0},{28,4},{1,25},{... | collective-permute-start | bytes 393224 | tf_op jit(solution)/shard_map/ppermute | solution.py:27
  45.9 7.8 %collective-permute-start.6 = (bf16[256,256]{1,0:T(8,128)(2,1)S(1)}, bf16[256,256]{1,0:T(8,128)(2,1)S(1)}, u32[]{:S(2)}, u32[]{:S(2)}) collective-permute-start(bf16[256,256]{1,0:T(8,128)(2,1)S(1)} %get-tuple-element.34), channel_id=1, source_target_pairs={{0,28},{4,24},{8,20},{12,16},{16,12},{20,8},{24,4},{28,0},{1,29},{... | collective-permute-start | bytes 393224 | tf_op jit(solution)/shard_map/ppermute | solution.py:27
  57.0 1.9 copy-start.14
  104.8 14.2 %copy-start.2 = (f32[256,128,32]{1,2,0:T(8,128)S(1)}, f32[256,128,32]{1,2,0:T(8,128)}, u32[]{:S(2)}) copy-start(f32[256,128,32]{1,2,0:T(8,128)} %fusion.166) | copy-start | bytes 12582916
  104.8 14.2 %copy-start.3 = (f32[256,128,32]{1,2,0:T(8,128)S(1)}, f32[256,128,32]{1,2,0:T(8,128)}, u32[]{:S(2)}) copy-start(f32[256,128,32]{1,2,0:T(8,128)} %fusion.158) | copy-start | bytes 12582916
  148.3 3.3 copy-start.8
  242.7 6.0 %copy-start.6 = (f32[256,32,128]{2,0,1:T(8,128)S(1)}, f32[256,32,128]{2,0,1:T(8,128)}, u32[]{:S(2)}) copy-start(f32[256,32,128]{2,0,1:T(8,128)} %get-tuple-element.20) | copy-start | bytes 12582916
  254.6 3.8 copy-start.4
  258.4 3.8 copy-start.5
  270.0 5.6 %copy-start.7 = (f32[256,32,128]{2,0,1:T(8,128)S(1)}, f32[256,32,128]{2,0,1:T(8,128)}, u32[]{:S(2)}) copy-start(f32[256,32,128]{2,0,1:T(8,128)} %get-tuple-element.21) | copy-start | bytes 12582916
  287.2 7.0 %copy-start.9 = (f32[256,32,128]{2,0,1:T(8,128)S(1)}, f32[256,32,128]{2,0,1:T(8,128)}, u32[]{:S(2)}) copy-start(f32[256,32,128]{2,0,1:T(8,128)} %get-tuple-element.43) | copy-start | bytes 12582916
  301.2 0.9 copy-start.12
  331.0 1.2 copy-start.15
  338.2 79.7 %all-to-all-start.1 = ((bf16[256,8,256]{0,2,1:T(8,128)(2,1)}), bf16[256,8,256]{0,2,1:T(8,128)(2,1)}, u32[]{:S(2)}, u32[]{:S(2)}) async-start(bf16[256,8,256]{0,2,1:T(8,128)(2,1)} %bitcast.19), calls=%async_computation.1 | async-start | bytes 2097152 | tf_op jit(solution)/shard_map/all_to_all | solution.py:148
  343.8 7.0 %copy-start.10 = (f32[256,32,128]{2,0,1:T(8,128)S(1)}, f32[256,32,128]{2,0,1:T(8,128)}, u32[]{:S(2)}) copy-start(f32[256,32,128]{2,0,1:T(8,128)} %get-tuple-element.24) | copy-start | bytes 12582916
  355.7 2.2 copy-start.11
  388.7 31.5 %copy-start.1 = (bf16[2048,128]{1,0:T(8,128)(2,1)S(1)}, bf16[2048,128]{1,0:T(8,128)(2,1)}, u32[]{:S(2)}) copy-start(bf16[2048,128]{1,0:T(8,128)(2,1)} %param.9) | copy-start | bytes 1572868
  (1 other events, 0.9 us)
